TPU v7x, 512 devices: a whole 4x4x16 slice. The times are simulated.
512 devices in a mesh: seq: 128 (over x, y, z_lo), head: 4 (over z_hi, core).
Axes of the slice: x: 4, y: 4, z: 16 (z_hi: 2, z_lo: 8; z = z_hi * 8 + z_lo), core: 2. Of those that a mesh axis runs over, the one named last changes fastest.
Arguments:
- tokens: bfloat16 [24576, 1024], P('seq'), may hold values from -6 to 6
- w_query: bfloat16 [1024, 512], P(None, 'head'), may hold values from -0.1875 to 0.1875
- w_key: bfloat16 [1024, 512], P(None, 'head'), may hold values from -0.1875 to 0.1875
- w_value: bfloat16 [1024, 512], P(None, 'head'), may hold values from -0.1875 to 0.1875
- w_out: bfloat16 [512, 1024], P('head'), may hold values from -0.25 to 0.25
- temper: float32 [4], replicated, may hold values from 3 to 6
Outputs:
- layer_out: bfloat16 [24576, 1024], P(('seq', 'head'))
All inputs are finite; a program needn't handle non-finite values.
Results may differ from a plain program's by a relative error of at most 0.015.
Values may be sent and summed in bfloat16 or wider, within the bound.
A program may use at most 128 MiB of HBM per device.

v0:
```python
import math

import jax
import jax.numpy as jnp
from jax import lax
from jax.sharding import PartitionSpec as P

HD = 128


EPS = 1e-06


def unit_rows(raw, heads):
    shaped = raw.reshape(raw.shape[0], heads, HD)
    shaped = shaped * lax.rsqrt(jnp.mean(shaped * shaped, axis=-1, keepdims=True) + EPS)
    return shaped.reshape(raw.shape[0], heads * HD).astype(jnp.bfloat16)


def make_fold(queries, scale, heads):
    rows_q = queries.shape[0]
    query_heads = queries.reshape(rows_q, heads, HD)

    def one_block(carry, pair):
        summed, total = carry
        key_block, value_block = pair
        width = key_block.shape[0]
        key_heads = key_block.reshape(width, heads, HD)
        value_heads = value_block.reshape(width, heads, HD)
        score = jnp.einsum(
            "qhd,khd->hqk", query_heads, key_heads, preferred_element_type=jnp.float32
        )
        weight = jnp.exp(score * scale[:, None, None])
        total = total + jnp.transpose(jnp.sum(weight, axis=-1))
        summed = summed + jnp.einsum(
            "hqk,khd->qhd",
            weight.astype(jnp.bfloat16),
            value_heads,
            preferred_element_type=jnp.float32,
        ).reshape(rows_q, heads * HD)
        return ((summed, total), None)

    def fold(carry, piece, start):
        key_piece, value_piece = piece
        count_rows = key_piece.shape[0]
        block = 512
        blocks = count_rows // block
        stacked = (
            key_piece.reshape(blocks, block, heads * HD),
            value_piece.reshape(blocks, block, heads * HD),
        )
        carry, unused = lax.scan(one_block, carry, stacked)
        return carry

    return fold


def finish(summed, total, heads):
    rows_q = summed.shape[0]
    return (
        (summed.reshape(rows_q, heads, HD) / total[:, :, None])
        .reshape(rows_q, heads * HD)
        .astype(jnp.bfloat16)
    )


def project_heads(attended, w_out):
    return lax.psum_scatter(
        jnp.dot(attended, w_out, preferred_element_type=jnp.float32).astype(jnp.bfloat16),
        "head",
        scatter_dimension=0,
        tiled=True,
    )


def on_device(tokens, w_query, w_key, w_value, w_out, temper):
    heads_dev = w_query.shape[1] // HD
    query_unit = unit_rows(jnp.dot(tokens, w_query, preferred_element_type=jnp.float32), heads_dev)
    key_unit = unit_rows(jnp.dot(tokens, w_key, preferred_element_type=jnp.float32), heads_dev)
    values = jnp.dot(tokens, w_value, preferred_element_type=jnp.float32).astype(jnp.bfloat16)
    scale = lax.dynamic_slice_in_dim(
        temper, lax.axis_index("head") * heads_dev, heads_dev
    ) / math.sqrt(HD)
    rows_q = query_unit.shape[0]
    start_carry = (
        jnp.zeros((rows_q, heads_dev * HD), jnp.float32),
        jnp.zeros((rows_q, heads_dev), jnp.float32),
    )
    summed, total = make_fold(query_unit, scale, heads_dev)(
        start_carry,
        (
            lax.all_gather(key_unit, "seq", axis=0, tiled=True),
            lax.all_gather(values, "seq", axis=0, tiled=True),
        ),
        jnp.int32(0),
    )
    attended = finish(summed, total, heads_dev)
    return project_heads(attended, w_out)


def solution(mesh):
    return jax.shard_map(
        on_device,
        mesh=mesh,
        in_specs=(
            P("seq", None),
            P(None, "head"),
            P(None, "head"),
            P(None, "head"),
            P("head", None),
            P(),
        ),
        out_specs=P(("seq", "head"), None),
        check_vma=False,
    )
```

profile of v0, /device:TPU:1, one launch (start us, length us, event | category | flops | bytes accessed | tf_op | source)
XLA Modules:
  0.0 2137.6 jit_solution(7991070718347004245)
XLA Ops:
  7.5 1.3 multiply_reduce_fusion.1
  9.6 1.8 convolution_convert_fusion.1
  11.6 1.3 dynamic_slice.10
  13.5 1.3 multiply_reduce_fusion
  14.9 895.7 %all-gather.5.cloned.1.call-done = bf16[24576,128]{1,0:T(8,128)(2,1)} async-done(((bf16[192,128]{1,0:T(8,128)(2,1)}), bf16[24576,128]{1,0:T(8,128)(2,1)}) %all-gather.5.cloned.1.call-update) | async-done | bytes 6291472 | tf_op jit(solution)/shard_map/all_gather | solution.py:92
  910.6 972.5 %all-gather.3.cloned.1.call-done = bf16[24576,128]{1,0:T(8,128)(2,1)} async-done(((bf16[192,128]{1,0:T(8,128)(2,1)}), bf16[24576,128]{1,0:T(8,128)(2,1)}) %all-gather.3.cloned.1.call-update) | async-done | bytes 6291472 | tf_op jit(solution)/shard_map/all_gather | solution.py:93
  1883.0 114.4 %while.13 = (s32[]{:T(128)}, f32[192,128]{1,0:T(8,128)S(1)}, f32[192,1]{0,1:T(1,128)S(1)}, bf16[48,512,128]{2,1,0:T(8,128)(2,1)}, bf16[48,512,128]{2,1,0:T(8,128...) while((s32[]{:T(128)}, f32[192,128]{1,0:T(8,128)S(1)}, ...), condition=%wide.region_4.5_spmd.clone, body=%wide.region_2.4_spmd.clone.sunk | while | flops 50675904 | bytes 905832 | solution.py:52
  1885.4 1.2 fusion.29
  1887.8 1.2 fusion.29
  1890.2 1.2 fusion.29
  1892.6 1.2 fusion.29
  1894.9 1.2 fusion.29
  1897.3 1.2 fusion.29
  1899.7 1.2 fusion.29
  1902.1 1.2 fusion.29
  1904.5 1.2 fusion.29
  1906.9 1.2 fusion.29
  1909.2 1.2 fusion.29
  1911.6 1.2 fusion.29
  1914.0 1.2 fusion.29
  1916.4 1.2 fusion.29
  1918.8 1.2 fusion.29
  1921.2 1.2 fusion.29
  1923.5 1.2 fusion.29
  1925.9 1.2 fusion.29
  1928.3 1.2 fusion.29
  1930.7 1.2 fusion.29
  1933.1 1.2 fusion.29
  1935.5 1.2 fusion.29
  1937.8 1.2 fusion.29
  1940.2 1.2 fusion.29
  1942.6 1.2 fusion.29
  1945.0 1.2 fusion.29
  1947.4 1.2 fusion.29
  1949.8 1.2 fusion.29
  1952.1 1.2 fusion.29
  1954.5 1.2 fusion.29
  1956.9 1.2 fusion.29
  1959.3 1.2 fusion.29
  1961.7 1.2 fusion.29
  1964.1 1.2 fusion.29
  1966.4 1.2 fusion.29
  1968.8 1.2 fusion.29
  1971.2 1.2 fusion.29
  1987.9 1.2 fusion.29
  1990.3 1.2 fusion.29
  1992.7 1.2 fusion.29
  1998.5 132.5 %reduce-scatter.2.cloned.1.call-done = bf16[48,1024]{1,0:T(8,128)(2,1)} async-done(((bf16[192,1024]{1,0:T(8,128)(2,1)}), bf16[48,1024]{1,0:T(8,128)(2,1)}) %reduce-scatter.2.cloned.1.call-update) | async-done | bytes 98320 | tf_op jit(solution)/shard_map/reduce_scatter | solution.py:68
  (121 shorter events, 66.7 us)
Async XLA Ops:
  6.5 1.0 copy-start
  6.5 1990.9 %copy-start.1 = (bf16[128,1024]{1,0:T(8,128)(2,1)S(1)}, bf16[128,1024]{1,0:T(8,128)(2,1)}, u32[]{:S(2)}) copy-start(bf16[128,1024]{1,0:T(8,128)(2,1)} %param.12) | copy-start | bytes 786436
  6.5 904.0 %all-gather.5.cloned.1.call-start = ((), (), s32[]{:S(2)}) async-start(), calls=%async_computation.2 | async-start | bytes 6340608 | tf_op jit(solution)/shard_map/all_gather | solution.py:92
  9.6 1873.5 %all-gather.3.cloned.1.call-start = ((), (), s32[]{:S(2)}) async-start(), calls=%async_computation.1 | async-start | bytes 6340608 | tf_op jit(solution)/shard_map/all_gather | solution.py:93
  11.5 2119.5 %reduce-scatter.2.cloned.1.call-start = ((), (), s32[]{:S(2)}) async-start(), calls=%async_computation.3 | async-start | bytes 491520 | tf_op jit(solution)/shard_map/reduce_scatter | solution.py:68
Sparse Core Ops, SparseCore 0:
  9.7 900.8 all-gather.4
  912.6 970.3 all-gather.2
  1998.6 132.3 reduce-scatter.1
where the time goes:
time: 2140 us
  waiting for transfers between devices  2000 us (93%)
  matrix products  118 us (6%)
    all_gather x1, waiting for transfers between devices, on_device(): lax.all_gather(values, 'seq', axis=0, tiled=True)  972 us
    all_gather x1, waiting for transfers between devices, on_device(): lax.all_gather(key_unit, 'seq', axis=0, tiled=True)  896 us
    reduce_scatter x1, waiting for transfers between devices, project_heads(): lax.psum_scatter(jnp.dot(attended, w_out, preferred_element_type=jnp.floa...  133 us
    dot_general x48, matrix products, one_block(): jnp.einsum('qhd,khd->hqk', query_heads, key_heads, preferred_element_type...  59.1 us
    dot_general x48, matrix products, one_block(): jnp.einsum('hqk,khd->qhd', weight.astype(jnp.bfloat16), value_heads, pref...  53.3 us
  transfers between devices with their start and end apart: 3, of which 3 were waited for; matrix products, arithmetic and copies ran while one was open for 0% of the time, Pallas kernels for 0%

commit v1 on v0

v1 whole, which is shorter than its diff:
```python
import functools
import math

import jax
import jax.numpy as jnp
from jax import lax
from jax.experimental import pallas as pl
from jax.experimental.pallas import tpu as pltpu
from jax.sharding import PartitionSpec as P

MESH = pl.DeviceIdType.MESH
HD = 128
EPS = 1e-06
ROWS = 192
PART = 48
NZ = 8
F32 = jnp.float32
BF16 = jnp.bfloat16


def unit_rows(raw):
    return (raw * lax.rsqrt(jnp.mean(raw * raw, axis=-1, keepdims=True) + EPS)).astype(BF16)


class Gather:
    ORDER = (0, -1, 1, 2)

    def __init__(self, own, view, place, x_first, number, sems, first_target, target):
        self.own, self.view, self.place, self.x_first, self.number = own, view, place, x_first, number
        self.d_recv, self.send_sem, self.recv_sem = sems
        self.first_target, self.target = first_target, target
        self.table = []
        for i in self.ORDER:
            self.table += [(i, 0, None, 1), (i, 0, None, -1), (i, -1, 0, 1), (i, 1, 1, -1)]

    def at(self, i, j):
        x, y = self.place
        dx, dy = (i, j) if self.x_first else (j, i)
        return lax.rem(x + dx + 8, 4), lax.rem(y + dy + 8, 4)

    def first(self, n, received=False):
        at = self.at(-n, 0) if received else self.place
        return pltpu.make_async_remote_copy(
            src_ref=self.own,
            dst_ref=self.view(*at, None),
            send_sem=self.send_sem.at[self.number],
            recv_sem=self.d_recv.at[self.number * 4 + n],
            device_id=self.first_target(*self.at(n, 0)),
            device_id_type=MESH,
        )

    def copy(self, k, received):
        i, j, part, step = self.table[k]
        ref = self.view(*self.at(i, j - step if received else j), part)
        return self.along(k, ref, self.at(0, step))

    def along(self, k, ref, to):
        return pltpu.make_async_remote_copy(
            src_ref=ref,
            dst_ref=ref,
            send_sem=self.send_sem.at[self.number],
            recv_sem=self.recv_sem.at[self.number * 16 + k],
            device_id=self.target(*to),
            device_id_type=MESH,
        )

    def first_got(self, i):
        self.first((-i) % 4, True).wait_recv()

    def start(self, *ks):
        for k in ks:
            self.copy(k, False).start()

    def got(self, *ks):
        for k in ks:
            self.copy(k, True).wait_recv()

    def sent(self, ref):
        self.along(0, ref, self.at(0, 1)).wait_send()


def kernel(
    tok_hbm, wq_hbm, wk_hbm, wv_hbm, wo_hbm, temper_hbm, out_ref,
    temper, tok, wq, wk, wv, wall, qst, kst, vst, qbuf, kbuf, vbuf, acc,
    xo, xt, go, gt, so, st, ro, rt,
    load_sem, d_recv, g_send, g_recv, m_send, m_recv, w_send, w_recv, x_send, x_recv,
    q_send, q_recv, f_send, f_recv, o_send, o_recv, t_send, t_recv,
):
    s, h = lax.axis_index("seq"), lax.axis_index("head")
    x, y, zl = lax.div(s, 32), lax.rem(lax.div(s, 8), 4), lax.rem(s, 8)
    zh, c = lax.div(h, 2), lax.rem(h, 2)
    p = lax.rem(zl, 2)
    near = lax.div(zl, 4)
    other = h + 1 - 2 * c
    across = lax.rem(h + 2, 4)
    column = s - zl
    mine = c == p
    z_first = jnp.where(mine, zl, zl + 1 - 2 * p)
    h_first = jnp.where(mine, h, other)

    def rdma(src, dst, send, recv, dev):
        return pltpu.make_async_remote_copy(
            src_ref=src, dst_ref=dst, send_sem=send, recv_sem=recv, device_id=dev, device_id_type=MESH
        )

    loads = [
        pltpu.make_async_copy(src, dst, load_sem.at[i])
        for i, (src, dst) in enumerate(
            [
                (tok_hbm, tok),
                (wk_hbm, wk),
                (wv_hbm, wv),
                (wq_hbm, wq),
                (wo_hbm, wall.at[pl.ds(pl.multiple_of(h * HD, HD), HD)]),
                (temper_hbm, temper),
            ]
        )
    ]
    for load in loads:
        load.start()

    barrier = pltpu.get_barrier_semaphore()

    def plane(px, py):
        return ((px * 4 + py) * 8 + zl, h)

    def first_plane(px, py):
        return ((px * 4 + py) * 8 + z_first, h_first)

    def greet_plane(where):
        for n in (1, 2, 3):
            for at in ((lax.rem(x + n, 4), y), (x, lax.rem(y + n, 4))):
                pl.semaphore_signal(barrier, inc=1, device_id=where(*at), device_id_type=MESH)

    greet_plane(plane)

    @pl.when(jnp.logical_not(mine))
    def _():
        greet_plane(first_plane)

    def greet(o, carry):
        at = lax.rem(zl * 4 + h + o, 32)
        pl.semaphore_signal(
            barrier, inc=1, device_id=(column + lax.div(at, 4), lax.rem(at, 4)), device_id_type=MESH
        )
        return carry

    lax.fori_loop(1, 32, greet, 0)
    acc[...] = jnp.zeros_like(acc)

    def rows_of(px, py, part):
        first = (py * 4 + px) * ROWS
        if part is None:
            return pl.ds(pl.multiple_of(first, ROWS), ROWS)
        return pl.ds(pl.multiple_of(first + part * (ROWS // 2), ROWS // 2), ROWS // 2)

    def k_view(px, py, part):
        return kbuf.at[rows_of(px, py, part)]

    def v_view(px, py, part):
        return vbuf.at[rows_of(px, py, part)]

    sems = (d_recv, g_send, g_recv)
    keys = Gather(kst, k_view, (x, y), True, 0, sems, first_plane, plane)
    vals = Gather(vst, v_view, (x, y), False, 1, sems, first_plane, plane)

    def head_rows(head):
        return wall.at[pl.ds(pl.multiple_of(head * HD, HD), HD)]

    def w_piece(head, px):
        first = pl.multiple_of(head * HD + lax.rem(px, 2) * 64, 64)
        lanes = pl.multiple_of((y * 2 + lax.div(px, 2)) * 128, 128)
        return wall.at[pl.ds(first, 64), pl.ds(lanes, 128)]

    def w_row(head, py):
        return wall.at[pl.ds(pl.multiple_of(head * HD, HD), HD), pl.ds(pl.multiple_of(py * 256, 256), 256)]

    def w_share_x(n, received=False):
        ref = w_piece(across, lax.rem(x + 4 - n, 4) if received else x)
        return rdma(ref, ref, w_send.at[0], w_recv.at[n], plane(lax.rem(x + n, 4), y))

    def w_share_y(n, received=False):
        ref = w_row(across, lax.rem(y + 4 - n, 4) if received else y)
        return rdma(ref, ref, w_send.at[1], w_recv.at[4 + n], plane(x, lax.rem(y + n, 4)))

    w_across = rdma(w_piece(h, x), w_piece(h, x), m_send.at[0], m_recv.at[0], (s, across))
    w_across_in = rdma(w_piece(across, x), w_piece(across, x), m_send.at[0], m_recv.at[0], (s, across))
    w_other = rdma(head_rows(h), head_rows(h), m_send.at[1], m_recv.at[1], (s, other))
    w_other_in = rdma(head_rows(other), head_rows(other), m_send.at[1], m_recv.at[1], (s, other))
    far_other = lax.rem(other + 2, 4)
    w_last = rdma(head_rows(across), head_rows(across), m_send.at[2], m_recv.at[2], (s, other))
    w_last_in = rdma(head_rows(far_other), head_rows(far_other), m_send.at[2], m_recv.at[2], (s, other))

    loads[0].wait()
    loads[1].wait()
    key_unit = unit_rows(jnp.dot(tok[...], wk[...], preferred_element_type=F32))
    kst[...] = key_unit

    @pl.when(mine)
    def _():
        kbuf[rows_of(x, y, None)] = key_unit
        pl.semaphore_wait(barrier, 37)

    @pl.when(jnp.logical_not(mine))
    def _():
        pl.semaphore_wait(barrier, 43)

    def give_first(g):
        for n in (1, 3, 2):
            g.first(n).start()

        @pl.when(jnp.logical_not(mine))
        def _():
            g.first(0).start()

        @pl.when(mine)
        def _():
            g.start(0, 1)

    give_first(keys)
    loads[4].wait()
    w_across.start()
    w_other.start()
    loads[2].wait()
    value = jnp.dot(tok[...], wv[...], preferred_element_type=F32).astype(BF16)
    vst[...] = value

    @pl.when(mine)
    def _():
        vbuf[rows_of(x, y, None)] = value

    give_first(vals)

    loads[3].wait()
    query_unit = unit_rows(jnp.dot(tok[...], wq[...], preferred_element_type=F32))
    qst[...] = query_unit

    def q_view(u):
        return qbuf.at[pl.ds(pl.multiple_of(u * ROWS, ROWS), ROWS)]

    half, bit = lax.div(zl, 4), lax.rem(lax.div(zl, 2), 2)
    q_targets = (half * 2 + bit, half * 2 + 1 - bit, 2 - half * 2 + bit, 3 - half * 2 - bit)
    q_self = jnp.logical_and(mine, near == c)

    def q_copy(n):
        return rdma(
            qst,
            q_view(zl),
            q_send.at[n],
            q_recv.at[lax.rem(zl, 4)],
            (column + c + 2 * q_targets[n], zh * 2 + near),
        )

    @pl.when(q_self)
    def _():
        qbuf[pl.ds(pl.multiple_of(zl * ROWS, ROWS), ROWS)] = query_unit

    @pl.when(jnp.logical_not(q_self))
    def _():
        q_copy(0).start()

    q_copy(1).start()
    loads[5].wait()

    @pl.when(jnp.logical_not(mine))
    def _():
        for g in (keys, vals):
            g.first_got(0)
            g.start(0, 1)

    for t, i in ((1, -1), (2, 1), (3, 2)):
        for g in (keys, vals):
            g.first_got(i)
            g.start(4 * t, 4 * t + 1)

    for n in (2, 3):
        q_copy(n).start()

    def relay(g, t):
        g.got(4 * t)
        g.start(4 * t + 2)
        g.got(4 * t + 1)
        g.start(4 * t + 3)

    for t in (0, 1, 2):
        for g in (keys, vals):
            relay(g, t)
    w_across_in.wait_recv()
    for n in (1, 3, 2):
        w_share_x(n).start()
    vals.got(2, 3)

    def unit_at(k):
        return k + near * (7 - 2 * k)

    def q_arrived(k):
        u = unit_at(k)
        slot = lax.rem(u, 4)
        first_core = (near == c) if k < 4 else (near != c)
        forward = rdma(q_view(u), q_view(u), f_send.at[slot], f_recv.at[slot], (s, other))
        direct = rdma(q_view(u), q_view(u), q_send.at[0], q_recv.at[slot], (s, other))

        @pl.when(first_core)
        def _():
            if k < 4:

                @pl.when(jnp.logical_not(jnp.logical_and(q_self, u == zl)))
                def _():
                    direct.wait_recv()
            else:
                direct.wait_recv()
            forward.start()

        @pl.when(jnp.logical_not(first_core))
        def _():
            forward.wait_recv()

    scale = temper[zh * 2 + p] * F32(math.log2(math.e) / math.sqrt(HD))

    ones = jnp.ones((4 * ROWS, HD), BF16)

    def piece(half, dy):
        q0 = pl.multiple_of(half * (4 * ROWS), 4 * ROWS)
        k0 = pl.multiple_of(lax.rem(y + dy, 4) * (4 * ROWS), 4 * ROWS)
        score = lax.dot_general(
            qbuf[pl.ds(q0, 4 * ROWS)],
            kbuf[pl.ds(k0, 4 * ROWS)],
            (((1,), (1,)), ((), ())),
            preferred_element_type=F32,
        )
        weight = jnp.exp2(score * scale).astype(BF16)
        value_block = jnp.concatenate([vbuf[pl.ds(k0, 4 * ROWS)], ones], axis=1)
        acc[pl.ds(q0, 4 * ROWS)] += jnp.dot(weight, value_block, preferred_element_type=F32)

    lane = lax.broadcasted_iota(jnp.int32, (PART, HD), 1)
    row = lax.broadcasted_iota(jnp.int32, (PART, HD), 0)
    diagonal = lane == row
    slot = (zh * 2 + p) * 4 + lax.div(zl, 2)

    def part_rows(core, i):
        return pl.ds(pl.multiple_of(core * (4 * ROWS) + i * PART, PART), PART)

    def give_copies(n):
        at = pl.ds(n * 4, 4)
        return (
            rdma(xo.at[at], go.at[at], x_send.at[0], x_recv.at[n], (s, other)),
            rdma(xt.at[at], gt.at[at], x_send.at[1], x_recv.at[4 + n], (s, other)),
        )

    def block_of(core, i):
        block = acc[part_rows(core, i)]
        return block[:, :HD], jnp.sum(jnp.where(diagonal, block[:, HD:], 0.0), axis=0, keepdims=True)

    def give(n, carry):
        def one(k, inner):
            i = n * 4 + k
            summed, xt[i] = block_of(1 - c, i)
            xo[i] = summed.astype(BF16)
            return inner

        lax.fori_loop(0, 4, one, 0)
        for copy in give_copies(n):
            copy.start()
        return carry

    def o_copy(i):
        dev = (column + c * 4 + lax.div(i, 4), lax.rem(i, 4))
        return (
            rdma(so.at[i], ro.at[slot], o_send, o_recv, dev),
            rdma(st.at[i], rt.at[slot], t_send, t_recv, dev),
        )

    def o_self(i):
        return jnp.logical_and(c * 4 + lax.div(i, 4) == zl, lax.rem(i, 4) == h)

    def settle(n, carry):
        for copy in give_copies(n):
            copy.wait_recv()

        def one(k, inner):
            i = n * 4 + k
            summed, total = block_of(c, i)
            summed, total = (summed + go[i].astype(F32)).astype(BF16), total + gt[i]
            so[i], st[i] = summed, total

            @pl.when(o_self(i))
            def _():
                ro[slot], rt[slot] = summed, total

            @pl.when(jnp.logical_not(o_self(i)))
            def _():
                for copy in o_copy(i):
                    copy.start()

            return inner

        lax.fori_loop(0, 4, one, 0)
        return carry

    def step(i, carry):
        def at(n, events):
            @pl.when(i == n)
            def _():
                events()

        def before_1():
            for g in (keys, vals):
                relay(g, 3)
            vals.got(6, 7)
            for n in (1, 3, 2):
                w_share_x(n, True).wait_recv()
            for n in (1, 3, 2):
                w_share_y(n).start()

        def before_2():
            vals.got(10, 11)

        def before_3():
            for k in range(4, 8):
                q_arrived(k)
            for n in (1, 3, 2):
                w_share_y(n, True).wait_recv()
            w_last.start()

        def before_6():
            keys.got(2, 3, 6, 7, 10, 11, 14, 15)
            vals.got(14, 15)

        def before_7():
            @pl.when(near != c)
            def _():
                lax.fori_loop(0, 4, give, 0)

        at(1, before_1)
        at(2, before_2)
        at(3, before_3)
        at(6, before_6)
        at(7, before_7)
        near_now = jnp.logical_or(i < 3, i == 6)
        r = jnp.where(i >= 6, 3, lax.rem(i, 3))
        piece(
            jnp.where(near_now, near, 1 - near),
            jnp.where(r == 0, 0, jnp.where(r == 1, 3, jnp.where(r == 2, 1, 2))),
        )
        return carry

    for k in range(4):
        q_arrived(k)
    lax.fori_loop(0, 8, step, 0)

    @pl.when(near == c)
    def _():
        lax.fori_loop(0, 4, give, 0)

    lax.fori_loop(0, 4, settle, 0)

    for g, ref in ((keys, kbuf), (vals, vbuf)):
        @pl.when(mine)
        def _():
            g.sent(ref.at[pl.ds(0, 15 * ROWS)])

        @pl.when(jnp.logical_not(mine))
        def _():
            g.sent(ref)

    for copy in (w_across, w_other, w_last):
        copy.wait_send()
    three_pieces = wall.at[pl.ds(0, 64), pl.ds(0, 384)]
    three_rows = wall.at[pl.ds(0, HD), pl.ds(0, 768)]
    rdma(three_pieces, three_pieces, w_send.at[0], w_recv.at[1], plane(lax.rem(x + 1, 4), y)).wait_send()
    rdma(three_rows, three_rows, w_send.at[1], w_recv.at[5], plane(x, lax.rem(y + 1, 4))).wait_send()
    rdma(xo, go, x_send.at[0], x_recv.at[0], (s, other)).wait_send()
    rdma(xt, gt, x_send.at[1], x_recv.at[4], (s, other)).wait_send()

    @pl.when(jnp.logical_not(q_self))
    def _():
        q_copy(0).wait_send()

    for n in (1, 2, 3):
        q_copy(n).wait_send()

    def forwarded(i, carry):
        rdma(q_view(c * 4 + i), q_view(c * 4 + i), f_send.at[i], f_recv.at[i], (s, other)).wait_send()
        return carry

    lax.fori_loop(0, 4, forwarded, 0)

    w_other_in.wait_recv()
    w_last_in.wait_recv()

    def all_parts(count):
        at = pl.ds(0, count)
        return (
            rdma(so.at[at], ro.at[at], o_send, o_recv, (s, other)),
            rdma(st.at[at], rt.at[at], t_send, t_recv, (s, other)),
        )

    @pl.when(near == c)
    def _():
        for copy in all_parts(15):
            copy.wait_recv()

    @pl.when(near != c)
    def _():
        for copy in all_parts(16):
            copy.wait_recv()

    attended = []
    for head in range(4):
        summed = sum(ro[head * 4 + j].astype(F32) for j in range(4))
        total = sum(rt[head * 4 + j] for j in range(4))
        total = jnp.sum(jnp.where(diagonal, jnp.broadcast_to(total, (PART, HD)), 0.0), axis=1, keepdims=True)
        attended.append((summed / total).astype(BF16))
    out_ref[...] = jnp.dot(
        jnp.concatenate(attended, axis=1), wall[...], preferred_element_type=F32
    ).astype(BF16)

    @pl.when(near == c)
    def _():
        for copy in all_parts(15):
            copy.wait_send()

    @pl.when(near != c)
    def _():
        for copy in all_parts(16):
            copy.wait_send()


def on_device(tokens, w_query, w_key, w_value, w_out, temper):
    dma = pltpu.SemaphoreType.DMA
    d_model = tokens.shape[1]
    return pl.pallas_call(
        kernel,
        out_shape=jax.ShapeDtypeStruct((PART, d_model), BF16),
        in_specs=[pl.BlockSpec(memory_space=pltpu.HBM)] * 6,
        out_specs=pl.BlockSpec(memory_space=pltpu.VMEM),
        scratch_shapes=[
            pltpu.SMEM((4,), F32),
            pltpu.VMEM((ROWS, d_model), BF16),
            pltpu.VMEM((d_model, HD), BF16),
            pltpu.VMEM((d_model, HD), BF16),
            pltpu.VMEM((d_model, HD), BF16),
            pltpu.VMEM((4 * HD, d_model), BF16),
            pltpu.VMEM((ROWS, HD), BF16),
            pltpu.VMEM((ROWS, HD), BF16),
            pltpu.VMEM((ROWS, HD), BF16),
            pltpu.VMEM((NZ * ROWS, HD), BF16),
            pltpu.VMEM((16 * ROWS, HD), BF16),
            pltpu.VMEM((16 * ROWS, HD), BF16),
            pltpu.VMEM((NZ * ROWS, 2 * HD), F32),
            pltpu.VMEM((16, PART, HD), BF16),
            pltpu.VMEM((16, 1, HD), F32),
            pltpu.VMEM((16, PART, HD), BF16),
            pltpu.VMEM((16, 1, HD), F32),
            pltpu.VMEM((16, PART, HD), BF16),
            pltpu.VMEM((16, 1, HD), F32),
            pltpu.VMEM((16, PART, HD), BF16),
            pltpu.VMEM((16, 1, HD), F32),
            dma((6,)),
            dma((8,)),
            dma((2,)),
            dma((32,)),
            dma((3,)),
            dma((3,)),
            dma((2,)),
            dma((8,)),
            dma((2,)),
            dma((8,)),
            dma((4,)),
            dma((4,)),
            dma((4,)),
            dma((4,)),
            dma(()),
            dma(()),
            dma(()),
            dma(()),
        ],
        compiler_params=pltpu.CompilerParams(
            collective_id=0, has_side_effects=True, vmem_limit_bytes=58 * 1024 * 1024
        ),
        name="layer",
    )(tokens, w_query, w_key, w_value, w_out, temper)


def solution(mesh):
    return jax.shard_map(
        on_device,
        mesh=mesh,
        in_specs=(
            P("seq", None),
            P(None, "head"),
            P(None, "head"),
            P(None, "head"),
            P("head", None),
            P(),
        ),
        out_specs=P(("seq", "head"), None),
        check_vma=False,
    )
```

time: 2140 us -> 61.5 us (0.03)
  waiting for transfers between devices: 2000 us -> 0 us
  matrix products: 118 us -> 0 us
  Pallas kernels: 0 us -> 59.4 us
    all_gather x2 -> x0, waiting for transfers between devices: 1870 us -> none  [the longest x1 972 us: on_device(): lax.all_gather(values, 'seq', axis=0, tiled=True)]
    reduce_scatter x1 -> x0, waiting for transfers between devices: 133 us -> none  [project_heads(): lax.psum_scatter(jnp.dot(attended, w_out, preferred_element_type=jnp.floa...]
    dot_general x100 -> x0, matrix products: 118 us -> none  [the longest x48 59.1 us: one_block(): jnp.einsum('qhd,khd->hqk', query_heads, key_heads, preferred_element_type...]
    pallas_call x0 -> x1, Pallas kernels: none -> 59.4 us  [on_device(): pl.pallas_call(kernel, out_shape=jax.ShapeDtypeStruct((PART, d_model), BF...]
  transfers between devices with their start and end apart: 3 -> 0, of which waited for: 3 -> 0; matrix products, arithmetic and copies ran while one was open for 0% -> 0% of each run, Pallas kernels for 0% -> 0%
where the time goes in v1:
time: 61.5 us; the launch traced here: 60.9 us
  Pallas kernels  59.4 us (97%)
  local copies, waits for them, and re-layouts  1.54 us (3%)
    pallas_call x1, Pallas kernels, on_device(): pl.pallas_call(kernel, out_shape=jax.ShapeDtypeStruct((PART, d_model), BF...  59.4 us
    unnamed x1, local copies, waits for them, and re-layouts  1.54 us

profile of v1, /device:TPU:1, one launch (start us, length us, event | category | flops | bytes accessed | tf_op | source)
XLA Modules:
  0.0 60.9 jit_solution(5750439239672020063)
XLA Ops:
  0.0 59.4 %layer.1 = bf16[48,1024]{1,0:T(8,128)(2,1)} custom-call(bf16[192,1024]{1,0:T(8,128)(2,1)} %tok_hbm.1, bf16[1024,128]{1,0:T(8,128)(2,1)} %wq_hbm.1, bf16[1024,128]{1,0:T(8,128)(2,1)} %wk_hbm.1, bf16[1024,128]{1,0:T(8,128)(2,1)} %wv_hbm.1, bf16[128,1024]{1,0:T(8,128)(2,1)} %wo_hbm.1, f32[4]{0:T(128)} %temper_hbm.1), custom_call_target="tpu_custom_call" | custom-call | tf_op jit(solution)/shard_map/layer/pallas_call | solution.py:532
  59.4 1.5 %copy.8 = bf16[48,1024]{1,0:T(8,128)(2,1)} copy(bf16[48,1024]{1,0:T(8,128)(2,1)} %layer.1) | data formatting | bytes 196608

commit v2 on v1

--- a/solution.py
+++ b/solution.py
@@ -81,10 +81,10 @@
 
 def kernel(
     tok_hbm, wq_hbm, wk_hbm, wv_hbm, wo_hbm, temper_hbm, out_ref,
-    temper, tok, wq, wk, wv, wall, qst, kst, vst, qbuf, kbuf, vbuf, acc,
+    temper, tok, wq, wkv, wall, qst, kvst, qbuf, kv_a, kv_b, acc,
     xo, xt, go, gt, so, st, ro, rt,
     load_sem, d_recv, g_send, g_recv, m_send, m_recv, w_send, w_recv, x_send, x_recv,
-    q_send, q_recv, f_send, f_recv, o_send, o_recv, t_send, t_recv,
+    q_send, q_recv, f_send, f_recv, o_send, o_recv, t_send, t_recv, ready,
 ):
     s, h = lax.axis_index("seq"), lax.axis_index("head")
     x, y, zl = lax.div(s, 32), lax.rem(lax.div(s, 8), 4), lax.rem(s, 8)
@@ -103,13 +103,45 @@
             src_ref=src, dst_ref=dst, send_sem=send, recv_sem=recv, device_id=dev, device_id_type=MESH
         )
 
+    barrier = pltpu.get_barrier_semaphore()
+
+    def plane(px, py):
+        return ((px * 4 + py) * 8 + zl, h)
+
+    def first_plane(px, py):
+        return ((px * 4 + py) * 8 + z_first, h_first)
+
+    def greet(dev):
+        pl.semaphore_signal(barrier, inc=1, device_id=dev, device_id_type=MESH)
+
+    def greet_plane(where):
+        for n in (1, 3, 2):
+            greet(where(lax.rem(x + n, 4), y))
+            greet(where(x, lax.rem(y + n, 4)))
+
+    q_self = jnp.logical_and(mine, near == c)
+
+    @pl.when(jnp.logical_not(mine))
+    def _():
+        greet_plane(first_plane)
+        greet(first_plane(x, y))
+
+    greet_plane(plane)
+    greet((s, other))
+    greet((s, across))
+    for n in range(4):
+
+        @pl.when(jnp.logical_not(jnp.logical_and(q_self, c * 4 + n == zl)))
+        def _():
+            greet((column + c * 4 + n, zh * 2 + p))
+
     loads = [
         pltpu.make_async_copy(src, dst, load_sem.at[i])
         for i, (src, dst) in enumerate(
             [
                 (tok_hbm, tok),
-                (wk_hbm, wk),
-                (wv_hbm, wv),
+                (wk_hbm, wkv.at[:, pl.ds(0, HD)]),
+                (wv_hbm, wkv.at[:, pl.ds(HD, HD)]),
                 (wq_hbm, wq),
                 (wo_hbm, wall.at[pl.ds(pl.multiple_of(h * HD, HD), HD)]),
                 (temper_hbm, temper),
@@ -119,50 +151,25 @@
     for load in loads:
         load.start()
 
-    barrier = pltpu.get_barrier_semaphore()
-
-    def plane(px, py):
-        return ((px * 4 + py) * 8 + zl, h)
-
-    def first_plane(px, py):
-        return ((px * 4 + py) * 8 + z_first, h_first)
-
-    def greet_plane(where):
-        for n in (1, 2, 3):
-            for at in ((lax.rem(x + n, 4), y), (x, lax.rem(y + n, 4))):
-                pl.semaphore_signal(barrier, inc=1, device_id=where(*at), device_id_type=MESH)
-
-    greet_plane(plane)
-
-    @pl.when(jnp.logical_not(mine))
-    def _():
-        greet_plane(first_plane)
-
-    def greet(o, carry):
-        at = lax.rem(zl * 4 + h + o, 32)
-        pl.semaphore_signal(
-            barrier, inc=1, device_id=(column + lax.div(at, 4), lax.rem(at, 4)), device_id_type=MESH
-        )
-        return carry
-
-    lax.fori_loop(1, 32, greet, 0)
     acc[...] = jnp.zeros_like(acc)
 
-    def rows_of(px, py, part):
-        first = (py * 4 + px) * ROWS
+    half_rows = ROWS // 2
+
+    def rows_of(at, part):
         if part is None:
-            return pl.ds(pl.multiple_of(first, ROWS), ROWS)
-        return pl.ds(pl.multiple_of(first + part * (ROWS // 2), ROWS // 2), ROWS // 2)
-
-    def k_view(px, py, part):
-        return kbuf.at[rows_of(px, py, part)]
-
-    def v_view(px, py, part):
-        return vbuf.at[rows_of(px, py, part)]
+            return pl.ds(pl.multiple_of(at * half_rows, half_rows), half_rows)
+        return pl.ds(pl.multiple_of(at * half_rows + part * PART, PART), PART)
+
+    def a_view(px, py, part):
+        return kv_a.at[rows_of(py * 4 + px, part)]
+
+    def b_view(px, py, part):
+        return kv_b.at[rows_of(px * 4 + py, part)]
 
     sems = (d_recv, g_send, g_recv)
-    keys = Gather(kst, k_view, (x, y), True, 0, sems, first_plane, plane)
-    vals = Gather(vst, v_view, (x, y), False, 1, sems, first_plane, plane)
+    along_x = Gather(kvst.at[pl.ds(0, half_rows)], a_view, (x, y), True, 0, sems, first_plane, plane)
+    along_y = Gather(kvst.at[pl.ds(half_rows, half_rows)], b_view, (x, y), False, 1, sems, first_plane, plane)
+    gathers = (along_x, along_y)
 
     def head_rows(head):
         return wall.at[pl.ds(pl.multiple_of(head * HD, HD), HD)]
@@ -193,17 +200,20 @@
 
     loads[0].wait()
     loads[1].wait()
-    key_unit = unit_rows(jnp.dot(tok[...], wk[...], preferred_element_type=F32))
-    kst[...] = key_unit
+    loads[2].wait()
+    raw = jnp.dot(tok[...], wkv[...], preferred_element_type=F32)
+    both = jnp.concatenate([unit_rows(raw[:, :HD]), raw[:, HD:].astype(BF16)], axis=1)
+    kvst[...] = both
 
     @pl.when(mine)
     def _():
-        kbuf[rows_of(x, y, None)] = key_unit
-        pl.semaphore_wait(barrier, 37)
+        kv_a[rows_of(y * 4 + x, None)] = both[:half_rows]
+        kv_b[rows_of(x * 4 + y, None)] = both[half_rows:]
+        pl.semaphore_wait(barrier, 12 - jnp.where(near == c, 1, 0))
 
     @pl.when(jnp.logical_not(mine))
     def _():
-        pl.semaphore_wait(barrier, 43)
+        pl.semaphore_wait(barrier, 19)
 
     def give_first(g):
         for n in (1, 3, 2):
@@ -217,20 +227,10 @@
         def _():
             g.start(0, 1)
 
-    give_first(keys)
+    give_first(along_x)
+    give_first(along_y)
     loads[4].wait()
     w_across.start()
-    w_other.start()
-    loads[2].wait()
-    value = jnp.dot(tok[...], wv[...], preferred_element_type=F32).astype(BF16)
-    vst[...] = value
-
-    @pl.when(mine)
-    def _():
-        vbuf[rows_of(x, y, None)] = value
-
-    give_first(vals)
-
     loads[3].wait()
     query_unit = unit_rows(jnp.dot(tok[...], wq[...], preferred_element_type=F32))
     qst[...] = query_unit
@@ -240,7 +240,6 @@
 
     half, bit = lax.div(zl, 4), lax.rem(lax.div(zl, 2), 2)
     q_targets = (half * 2 + bit, half * 2 + 1 - bit, 2 - half * 2 + bit, 3 - half * 2 - bit)
-    q_self = jnp.logical_and(mine, near == c)
 
     def q_copy(n):
         return rdma(
@@ -261,15 +260,16 @@
 
     q_copy(1).start()
     loads[5].wait()
+    w_other.start()
 
     @pl.when(jnp.logical_not(mine))
     def _():
-        for g in (keys, vals):
+        for g in gathers:
             g.first_got(0)
             g.start(0, 1)
 
     for t, i in ((1, -1), (2, 1), (3, 2)):
-        for g in (keys, vals):
+        for g in gathers:
             g.first_got(i)
             g.start(4 * t, 4 * t + 1)
 
@@ -281,14 +281,6 @@
         g.start(4 * t + 2)
         g.got(4 * t + 1)
         g.start(4 * t + 3)
-
-    for t in (0, 1, 2):
-        for g in (keys, vals):
-            relay(g, t)
-    w_across_in.wait_recv()
-    for n in (1, 3, 2):
-        w_share_x(n).start()
-    vals.got(2, 3)
 
     def unit_at(k):
         return k + near * (7 - 2 * k)
@@ -319,17 +311,17 @@
 
     ones = jnp.ones((4 * ROWS, HD), BF16)
 
-    def piece(half, dy):
+    def piece(half, d):
         q0 = pl.multiple_of(half * (4 * ROWS), 4 * ROWS)
-        k0 = pl.multiple_of(lax.rem(y + dy, 4) * (4 * ROWS), 4 * ROWS)
+        a0 = pl.multiple_of(lax.rem(y + d, 4) * (2 * ROWS), 2 * ROWS)
+        b0 = pl.multiple_of(lax.rem(x + d, 4) * (2 * ROWS), 2 * ROWS)
+        both_k = jnp.concatenate([kv_a[pl.ds(a0, 2 * ROWS), :HD], kv_b[pl.ds(b0, 2 * ROWS), :HD]], axis=0)
+        both_v = jnp.concatenate([kv_a[pl.ds(a0, 2 * ROWS), HD:], kv_b[pl.ds(b0, 2 * ROWS), HD:]], axis=0)
         score = lax.dot_general(
-            qbuf[pl.ds(q0, 4 * ROWS)],
-            kbuf[pl.ds(k0, 4 * ROWS)],
-            (((1,), (1,)), ((), ())),
-            preferred_element_type=F32,
+            qbuf[pl.ds(q0, 4 * ROWS)], both_k, (((1,), (1,)), ((), ())), preferred_element_type=F32
         )
         weight = jnp.exp2(score * scale).astype(BF16)
-        value_block = jnp.concatenate([vbuf[pl.ds(k0, 4 * ROWS)], ones], axis=1)
+        value_block = jnp.concatenate([both_v, ones], axis=1)
         acc[pl.ds(q0, 4 * ROWS)] += jnp.dot(weight, value_block, preferred_element_type=F32)
 
     lane = lax.broadcasted_iota(jnp.int32, (PART, HD), 1)
@@ -404,27 +396,27 @@
                 events()
 
         def before_1():
-            for g in (keys, vals):
-                relay(g, 3)
-            vals.got(6, 7)
+            for t in range(4):
+                for g in gathers:
+                    relay(g, t)
+            w_across_in.wait_recv()
+            for n in (1, 3, 2):
+                w_share_x(n).start()
+
+        def before_3():
+            for k in range(4, 8):
+                q_arrived(k)
+            pl.semaphore_signal(ready, inc=1, device_id=(s, across), device_id_type=MESH)
             for n in (1, 3, 2):
                 w_share_x(n, True).wait_recv()
             for n in (1, 3, 2):
                 w_share_y(n).start()
 
-        def before_2():
-            vals.got(10, 11)
-
-        def before_3():
-            for k in range(4, 8):
-                q_arrived(k)
+        def before_6():
+            for g in gathers:
+                g.got(2, 3, 6, 7, 10, 11, 14, 15)
             for n in (1, 3, 2):
                 w_share_y(n, True).wait_recv()
-            w_last.start()
-
-        def before_6():
-            keys.got(2, 3, 6, 7, 10, 11, 14, 15)
-            vals.got(14, 15)
 
         def before_7():
             @pl.when(near != c)
@@ -432,7 +424,6 @@
                 lax.fori_loop(0, 4, give, 0)
 
         at(1, before_1)
-        at(2, before_2)
         at(3, before_3)
         at(6, before_6)
         at(7, before_7)
@@ -452,12 +443,14 @@
     def _():
         lax.fori_loop(0, 4, give, 0)
 
+    w_last.start()
+    pl.semaphore_wait(ready, 1)
     lax.fori_loop(0, 4, settle, 0)
 
-    for g, ref in ((keys, kbuf), (vals, vbuf)):
+    for g, ref in ((along_x, kv_a), (along_y, kv_b)):
         @pl.when(mine)
         def _():
-            g.sent(ref.at[pl.ds(0, 15 * ROWS)])
+            g.sent(ref.at[pl.ds(0, 15 * half_rows)])
 
         @pl.when(jnp.logical_not(mine))
         def _():
@@ -528,6 +521,10 @@
 
 def on_device(tokens, w_query, w_key, w_value, w_out, temper):
     dma = pltpu.SemaphoreType.DMA
+    args = [
+        pltpu.with_memory_space_constraint(a, pltpu.HBM)
+        for a in (tokens, w_query, w_key, w_value, w_out, temper)
+    ]
     d_model = tokens.shape[1]
     return pl.pallas_call(
         kernel,
@@ -538,15 +535,13 @@
             pltpu.SMEM((4,), F32),
             pltpu.VMEM((ROWS, d_model), BF16),
             pltpu.VMEM((d_model, HD), BF16),
-            pltpu.VMEM((d_model, HD), BF16),
-            pltpu.VMEM((d_model, HD), BF16),
+            pltpu.VMEM((d_model, 2 * HD), BF16),
             pltpu.VMEM((4 * HD, d_model), BF16),
             pltpu.VMEM((ROWS, HD), BF16),
-            pltpu.VMEM((ROWS, HD), BF16),
-            pltpu.VMEM((ROWS, HD), BF16),
+            pltpu.VMEM((ROWS, 2 * HD), BF16),
             pltpu.VMEM((NZ * ROWS, HD), BF16),
-            pltpu.VMEM((16 * ROWS, HD), BF16),
-            pltpu.VMEM((16 * ROWS, HD), BF16),
+            pltpu.VMEM((8 * ROWS, 2 * HD), BF16),
+            pltpu.VMEM((8 * ROWS, 2 * HD), BF16),
             pltpu.VMEM((NZ * ROWS, 2 * HD), F32),
             pltpu.VMEM((16, PART, HD), BF16),
             pltpu.VMEM((16, 1, HD), F32),
@@ -574,12 +569,13 @@
             dma(()),
             dma(()),
             dma(()),
+            pltpu.SemaphoreType.REGULAR,
         ],
         compiler_params=pltpu.CompilerParams(
-            collective_id=0, has_side_effects=True, vmem_limit_bytes=58 * 1024 * 1024
+            collective_id=0, has_side_effects=True, vmem_limit_bytes=40 * 1024 * 1024
         ),
         name="layer",
-    )(tokens, w_query, w_key, w_value, w_out, temper)
+    )(*args)
 
 
 def solution(mesh):

time: 61.5 us -> 57.4 us (0.933)
  Pallas kernels: 59.4 us -> 55.7 us
  local copies, waits for them, and re-layouts: 1.54 us -> 0.64 us
    pallas_call x1, Pallas kernels: 59.4 us -> 55.7 us  [on_device(): pl.pallas_call(kernel, out_shape=jax.ShapeDtypeStruct((PART, d_model), BF...]
    unnamed x1, local copies, waits for them, and re-layouts: 1.54 us -> 0.64 us
where the time goes in v2:
time: 57.4 us; the launch traced here: 56.3 us
  Pallas kernels  55.7 us (97%)
  local copies, waits for them, and re-layouts  0.64 us (1%)
    pallas_call x1, Pallas kernels, on_device(): pl.pallas_call(kernel, out_shape=jax.ShapeDtypeStruct((PART, d_model), BF...  55.7 us

profile of v2, /device:TPU:1, one launch (start us, length us, event | category | flops | bytes accessed | tf_op | source)
XLA Modules:
  0.0 56.3 jit_solution(3647598101770009791)
XLA Ops:
  0.0 55.7 %layer.1 = bf16[48,1024]{1,0:T(8,128)(2,1)S(1)} custom-call(bf16[192,1024]{1,0:T(8,128)(2,1)} %tok_hbm.1, bf16[1024,128]{1,0:T(8,128)(2,1)} %wq_hbm.1, bf16[1024,128]{1,0:T(8,128)(2,1)} %wk_hbm.1, bf16[1024,128]{1,0:T(8,128)(2,1)} %wv_hbm.1, bf16[128,1024]{1,0:T(8,128)(2,1)} %wo_hbm.1, f32[4]{0:T(128)} %temper_hbm.1), custom_call_target="tpu_custom_call" | custom-call | tf_op jit(solution)/shard_map/layer/pallas_call | solution.py:529
  55.7 0.6 %copy.8 = bf16[48,1024]{1,0:T(8,128)(2,1)} copy(bf16[48,1024]{1,0:T(8,128)(2,1)S(1)} %layer.1) | data formatting | bytes 196608

commit v3 on v2

--- a/solution.py
+++ b/solution.py
@@ -333,7 +333,7 @@
         return pl.ds(pl.multiple_of(core * (4 * ROWS) + i * PART, PART), PART)
 
     def give_copies(n):
-        at = pl.ds(n * 4, 4)
+        at = pl.ds(pl.multiple_of(n * 4, 4), 4)
         return (
             rdma(xo.at[at], go.at[at], x_send.at[0], x_recv.at[n], (s, other)),
             rdma(xt.at[at], gt.at[at], x_send.at[1], x_recv.at[4 + n], (s, other)),
@@ -343,7 +343,12 @@
         block = acc[part_rows(core, i)]
         return block[:, :HD], jnp.sum(jnp.where(diagonal, block[:, HD:], 0.0), axis=0, keepdims=True)
 
-    def give(n, carry):
+    def turn(n):
+        return lax.rem(n + zl, 4)
+
+    def give(m, carry):
+        n = turn(m)
+
         def one(k, inner):
             i = n * 4 + k
             summed, xt[i] = block_of(1 - c, i)
@@ -365,7 +370,8 @@
     def o_self(i):
         return jnp.logical_and(c * 4 + lax.div(i, 4) == zl, lax.rem(i, 4) == h)
 
-    def settle(n, carry):
+    def settle(m, carry):
+        n = turn(m)
         for copy in give_copies(n):
             copy.wait_recv()
 
@@ -404,33 +410,42 @@
                 w_share_x(n).start()
 
         def before_3():
-            for k in range(4, 8):
-                q_arrived(k)
-            pl.semaphore_signal(ready, inc=1, device_id=(s, across), device_id_type=MESH)
+            for g in gathers:
+                g.got(2, 3, 6, 7, 10, 11, 14, 15)
             for n in (1, 3, 2):
                 w_share_x(n, True).wait_recv()
             for n in (1, 3, 2):
                 w_share_y(n).start()
 
-        def before_6():
-            for g in gathers:
-                g.got(2, 3, 6, 7, 10, 11, 14, 15)
-            for n in (1, 3, 2):
-                w_share_y(n, True).wait_recv()
-
-        def before_7():
+        def before_4():
             @pl.when(near != c)
             def _():
                 lax.fori_loop(0, 4, give, 0)
 
+            for k in range(4, 8):
+                q_arrived(k)
+            pl.semaphore_signal(ready, inc=1, device_id=(s, across), device_id_type=MESH)
+
+        def before_5():
+            for n in (1, 3, 2):
+                w_share_y(n, True).wait_recv()
+            w_last.start()
+
+        def before_6():
+            pl.semaphore_wait(ready, 1)
+
+            @pl.when(near == c)
+            def _():
+                lax.fori_loop(0, 4, settle, 0)
+
         at(1, before_1)
         at(3, before_3)
+        at(4, before_4)
+        at(5, before_5)
         at(6, before_6)
-        at(7, before_7)
-        near_now = jnp.logical_or(i < 3, i == 6)
-        r = jnp.where(i >= 6, 3, lax.rem(i, 3))
+        r = lax.rem(i, 4)
         piece(
-            jnp.where(near_now, near, 1 - near),
+            jnp.where(i < 4, near, 1 - near),
             jnp.where(r == 0, 0, jnp.where(r == 1, 3, jnp.where(r == 2, 1, 2))),
         )
         return carry
@@ -443,9 +458,9 @@
     def _():
         lax.fori_loop(0, 4, give, 0)
 
-    w_last.start()
-    pl.semaphore_wait(ready, 1)
-    lax.fori_loop(0, 4, settle, 0)
+    @pl.when(near != c)
+    def _():
+        lax.fori_loop(0, 4, settle, 0)
 
     for g, ref in ((along_x, kv_a), (along_y, kv_b)):
         @pl.when(mine)

time: 57.4 us -> 58.8 us (1.024)
  Pallas kernels: 55.7 us -> 57.3 us
    pallas_call x1, Pallas kernels: 55.7 us -> 57.3 us  [on_device(): pl.pallas_call(kernel, out_shape=jax.ShapeDtypeStruct((PART, d_model), BF...]
where the time goes in v3:
time: 58.8 us; the launch traced here: 58 us
  Pallas kernels  57.3 us (97%)
  local copies, waits for them, and re-layouts  0.64 us (1%)
    pallas_call x1, Pallas kernels, on_device(): pl.pallas_call(kernel, out_shape=jax.ShapeDtypeStruct((PART, d_model), BF...  57.3 us

profile of v3, /device:TPU:1, one launch (start us, length us, event | category | flops | bytes accessed | tf_op | source)
XLA Modules:
  0.0 58.0 jit_solution(13568033107644941506)
XLA Ops:
  0.0 57.3 %layer.1 = bf16[48,1024]{1,0:T(8,128)(2,1)S(1)} custom-call(bf16[192,1024]{1,0:T(8,128)(2,1)} %tok_hbm.1, bf16[1024,128]{1,0:T(8,128)(2,1)} %wq_hbm.1, bf16[1024,128]{1,0:T(8,128)(2,1)} %wk_hbm.1, bf16[1024,128]{1,0:T(8,128)(2,1)} %wv_hbm.1, bf16[128,1024]{1,0:T(8,128)(2,1)} %wo_hbm.1, f32[4]{0:T(128)} %temper_hbm.1), custom_call_target="tpu_custom_call" | custom-call | tf_op jit(solution)/shard_map/layer/pallas_call | solution.py:544
  57.4 0.6 %copy.8 = bf16[48,1024]{1,0:T(8,128)(2,1)} copy(bf16[48,1024]{1,0:T(8,128)(2,1)S(1)} %layer.1) | data formatting | bytes 196608

commit v4 on v2

--- a/solution.py
+++ b/solution.py
@@ -25,10 +25,10 @@
 class Gather:
     ORDER = (0, -1, 1, 2)
 
-    def __init__(self, own, view, place, x_first, number, sems, first_target, target):
+    def __init__(self, own, view, place, x_first, number, sems, target):
         self.own, self.view, self.place, self.x_first, self.number = own, view, place, x_first, number
         self.d_recv, self.send_sem, self.recv_sem = sems
-        self.first_target, self.target = first_target, target
+        self.target = target
         self.table = []
         for i in self.ORDER:
             self.table += [(i, 0, None, 1), (i, 0, None, -1), (i, -1, 0, 1), (i, 1, 1, -1)]
@@ -45,7 +45,7 @@
             dst_ref=self.view(*at, None),
             send_sem=self.send_sem.at[self.number],
             recv_sem=self.d_recv.at[self.number * 4 + n],
-            device_id=self.first_target(*self.at(n, 0)),
+            device_id=self.target(*self.at(n, 0)),
             device_id_type=MESH,
         )
 
@@ -81,7 +81,7 @@
 
 def kernel(
     tok_hbm, wq_hbm, wk_hbm, wv_hbm, wo_hbm, temper_hbm, out_ref,
-    temper, tok, wq, wkv, wall, qst, kvst, qbuf, kv_a, kv_b, acc,
+    temper, tok, wq, wkv, wall, qst, kvst, kvown, qbuf, kv_a, kv_b, acc,
     xo, xt, go, gt, so, st, ro, rt,
     load_sem, d_recv, g_send, g_recv, m_send, m_recv, w_send, w_recv, x_send, x_recv,
     q_send, q_recv, f_send, f_recv, o_send, o_recv, t_send, t_recv, ready,
@@ -95,8 +95,6 @@
     across = lax.rem(h + 2, 4)
     column = s - zl
     mine = c == p
-    z_first = jnp.where(mine, zl, zl + 1 - 2 * p)
-    h_first = jnp.where(mine, h, other)
 
     def rdma(src, dst, send, recv, dev):
         return pltpu.make_async_remote_copy(
@@ -108,25 +106,20 @@
     def plane(px, py):
         return ((px * 4 + py) * 8 + zl, h)
 
-    def first_plane(px, py):
-        return ((px * 4 + py) * 8 + z_first, h_first)
-
     def greet(dev):
         pl.semaphore_signal(barrier, inc=1, device_id=dev, device_id_type=MESH)
 
-    def greet_plane(where):
-        for n in (1, 3, 2):
-            greet(where(lax.rem(x + n, 4), y))
-            greet(where(x, lax.rem(y + n, 4)))
-
     q_self = jnp.logical_and(mine, near == c)
 
+    swap_to = (s + 1 - 2 * p, other)
+
     @pl.when(jnp.logical_not(mine))
     def _():
-        greet_plane(first_plane)
-        greet(first_plane(x, y))
-
-    greet_plane(plane)
+        greet(swap_to)
+
+    for n in (1, 3, 2):
+        greet(plane(lax.rem(x + n, 4), y))
+        greet(plane(x, lax.rem(y + n, 4)))
     greet((s, other))
     greet((s, across))
     for n in range(4):
@@ -167,8 +160,8 @@
         return kv_b.at[rows_of(px * 4 + py, part)]
 
     sems = (d_recv, g_send, g_recv)
-    along_x = Gather(kvst.at[pl.ds(0, half_rows)], a_view, (x, y), True, 0, sems, first_plane, plane)
-    along_y = Gather(kvst.at[pl.ds(half_rows, half_rows)], b_view, (x, y), False, 1, sems, first_plane, plane)
+    along_x = Gather(kvown.at[pl.ds(0, half_rows)], a_view, (x, y), True, 0, sems, plane)
+    along_y = Gather(kvown.at[pl.ds(half_rows, half_rows)], b_view, (x, y), False, 1, sems, plane)
     gathers = (along_x, along_y)
 
     def head_rows(head):
@@ -203,32 +196,32 @@
     loads[2].wait()
     raw = jnp.dot(tok[...], wkv[...], preferred_element_type=F32)
     both = jnp.concatenate([unit_rows(raw[:, :HD]), raw[:, HD:].astype(BF16)], axis=1)
-    kvst[...] = both
+    kv_swap = rdma(kvst, kvown, m_send.at[3], m_recv.at[3], swap_to)
+
+    def give_first():
+        for g in gathers:
+            for n in (1, 3, 2):
+                g.first(n).start()
+        for g in gathers:
+            g.start(0, 1)
+
+    def place_own(block):
+        kv_a[rows_of(y * 4 + x, None)] = block[:half_rows]
+        kv_b[rows_of(x * 4 + y, None)] = block[half_rows:]
 
     @pl.when(mine)
     def _():
-        kv_a[rows_of(y * 4 + x, None)] = both[:half_rows]
-        kv_b[rows_of(x * 4 + y, None)] = both[half_rows:]
+        kvown[...] = both
+        place_own(both)
         pl.semaphore_wait(barrier, 12 - jnp.where(near == c, 1, 0))
+        give_first()
 
     @pl.when(jnp.logical_not(mine))
     def _():
-        pl.semaphore_wait(barrier, 19)
-
-    def give_first(g):
-        for n in (1, 3, 2):
-            g.first(n).start()
-
-        @pl.when(jnp.logical_not(mine))
-        def _():
-            g.first(0).start()
-
-        @pl.when(mine)
-        def _():
-            g.start(0, 1)
-
-    give_first(along_x)
-    give_first(along_y)
+        kvst[...] = both
+        pl.semaphore_wait(barrier, 13)
+        kv_swap.start()
+
     loads[4].wait()
     w_across.start()
     loads[3].wait()
@@ -264,9 +257,9 @@
 
     @pl.when(jnp.logical_not(mine))
     def _():
-        for g in gathers:
-            g.first_got(0)
-            g.start(0, 1)
+        kv_swap.wait_recv()
+        place_own(kvown[...])
+        give_first()
 
     for t, i in ((1, -1), (2, 1), (3, 2)):
         for g in gathers:
@@ -333,7 +326,7 @@
         return pl.ds(pl.multiple_of(core * (4 * ROWS) + i * PART, PART), PART)
 
     def give_copies(n):
-        at = pl.ds(n * 4, 4)
+        at = pl.ds(pl.multiple_of(n * 4, 4), 4)
         return (
             rdma(xo.at[at], go.at[at], x_send.at[0], x_recv.at[n], (s, other)),
             rdma(xt.at[at], gt.at[at], x_send.at[1], x_recv.at[4 + n], (s, other)),
@@ -343,7 +336,12 @@
         block = acc[part_rows(core, i)]
         return block[:, :HD], jnp.sum(jnp.where(diagonal, block[:, HD:], 0.0), axis=0, keepdims=True)
 
-    def give(n, carry):
+    def turn(n):
+        return lax.rem(n + zl, 4)
+
+    def give(m, carry):
+        n = turn(m)
+
         def one(k, inner):
             i = n * 4 + k
             summed, xt[i] = block_of(1 - c, i)
@@ -365,7 +363,8 @@
     def o_self(i):
         return jnp.logical_and(c * 4 + lax.div(i, 4) == zl, lax.rem(i, 4) == h)
 
-    def settle(n, carry):
+    def settle(m, carry):
+        n = turn(m)
         for copy in give_copies(n):
             copy.wait_recv()
 
@@ -396,7 +395,7 @@
                 events()
 
         def before_1():
-            for t in range(4):
+            for t in (1, 2, 3):
                 for g in gathers:
                     relay(g, t)
             w_across_in.wait_recv()
@@ -412,11 +411,13 @@
             for n in (1, 3, 2):
                 w_share_y(n).start()
 
+        def before_5():
+            for n in (1, 3, 2):
+                w_share_y(n, True).wait_recv()
+
         def before_6():
             for g in gathers:
                 g.got(2, 3, 6, 7, 10, 11, 14, 15)
-            for n in (1, 3, 2):
-                w_share_y(n, True).wait_recv()
 
         def before_7():
             @pl.when(near != c)
@@ -425,6 +426,7 @@
 
         at(1, before_1)
         at(3, before_3)
+        at(5, before_5)
         at(6, before_6)
         at(7, before_7)
         near_now = jnp.logical_or(i < 3, i == 6)
@@ -435,6 +437,8 @@
         )
         return carry
 
+    for g in gathers:
+        relay(g, 0)
     for k in range(4):
         q_arrived(k)
     lax.fori_loop(0, 8, step, 0)
@@ -448,13 +452,11 @@
     lax.fori_loop(0, 4, settle, 0)
 
     for g, ref in ((along_x, kv_a), (along_y, kv_b)):
-        @pl.when(mine)
-        def _():
-            g.sent(ref.at[pl.ds(0, 15 * half_rows)])
-
-        @pl.when(jnp.logical_not(mine))
-        def _():
-            g.sent(ref)
+        g.sent(ref.at[pl.ds(0, 15 * half_rows)])
+
+    @pl.when(jnp.logical_not(mine))
+    def _():
+        kv_swap.wait_send()
 
     for copy in (w_across, w_other, w_last):
         copy.wait_send()
@@ -539,6 +541,7 @@
             pltpu.VMEM((4 * HD, d_model), BF16),
             pltpu.VMEM((ROWS, HD), BF16),
             pltpu.VMEM((ROWS, 2 * HD), BF16),
+            pltpu.VMEM((ROWS, 2 * HD), BF16),
             pltpu.VMEM((NZ * ROWS, HD), BF16),
             pltpu.VMEM((8 * ROWS, 2 * HD), BF16),
             pltpu.VMEM((8 * ROWS, 2 * HD), BF16),
@@ -555,8 +558,8 @@
             dma((8,)),
             dma((2,)),
             dma((32,)),
-            dma((3,)),
-            dma((3,)),
+            dma((4,)),
+            dma((4,)),
             dma((2,)),
             dma((8,)),
             dma((2,)),

time: 57.4 us -> 57.2 us (level); the launches traced: 56.3 us -> 57.1 us
  Pallas kernels: 55.7 us -> 56.4 us
    pallas_call x1, Pallas kernels: 55.7 us -> 56.4 us  [on_device(): pl.pallas_call(kernel, out_shape=jax.ShapeDtypeStruct((PART, d_model), BF...]
where the time goes in v4:
time: 57.2 us; the launch traced here: 57.1 us
  Pallas kernels  56.4 us (99%)
  local copies, waits for them, and re-layouts  0.64 us (1%)
    pallas_call x1, Pallas kernels, on_device(): pl.pallas_call(kernel, out_shape=jax.ShapeDtypeStruct((PART, d_model), BF...  56.4 us

profile of v4, /device:TPU:1, one launch (start us, length us, event | category | flops | bytes accessed | tf_op | source)
XLA Modules:
  0.0 57.1 jit_solution(17072497063828984786)
XLA Ops:
  0.0 56.4 %layer.1 = bf16[48,1024]{1,0:T(8,128)(2,1)S(1)} custom-call(bf16[192,1024]{1,0:T(8,128)(2,1)} %tok_hbm.1, bf16[1024,128]{1,0:T(8,128)(2,1)} %wq_hbm.1, bf16[1024,128]{1,0:T(8,128)(2,1)} %wk_hbm.1, bf16[1024,128]{1,0:T(8,128)(2,1)} %wv_hbm.1, bf16[128,1024]{1,0:T(8,128)(2,1)} %wo_hbm.1, f32[4]{0:T(128)} %temper_hbm.1), custom_call_target="tpu_custom_call" | custom-call | tf_op jit(solution)/shard_map/layer/pallas_call | solution.py:531
  56.4 0.6 %copy.8 = bf16[48,1024]{1,0:T(8,128)(2,1)} copy(bf16[48,1024]{1,0:T(8,128)(2,1)S(1)} %layer.1) | data formatting | bytes 196608

commit v5 on v4

--- a/solution.py
+++ b/solution.py
@@ -420,16 +420,14 @@
                 g.got(2, 3, 6, 7, 10, 11, 14, 15)
 
         def before_7():
-            @pl.when(near != c)
-            def _():
-                lax.fori_loop(0, 4, give, 0)
+            lax.fori_loop(0, 4, give, 0)
 
         at(1, before_1)
         at(3, before_3)
         at(5, before_5)
         at(6, before_6)
         at(7, before_7)
-        near_now = jnp.logical_or(i < 3, i == 6)
+        near_now = jnp.logical_or(i < 3, i == jnp.where(near == c, 7, 6))
         r = jnp.where(i >= 6, 3, lax.rem(i, 3))
         piece(
             jnp.where(near_now, near, 1 - near),
@@ -442,10 +440,6 @@
     for k in range(4):
         q_arrived(k)
     lax.fori_loop(0, 8, step, 0)
-
-    @pl.when(near == c)
-    def _():
-        lax.fori_loop(0, 4, give, 0)
 
     w_last.start()
     pl.semaphore_wait(ready, 1)

time: 57.2 us -> 56.5 us (0.988)
  Pallas kernels: 56.4 us -> 55.7 us
    pallas_call x1, Pallas kernels: 56.4 us -> 55.7 us  [on_device(): pl.pallas_call(kernel, out_shape=jax.ShapeDtypeStruct((PART, d_model), BF...]
where the time goes in v5:
time: 56.5 us; the launch traced here: 56.4 us
  Pallas kernels  55.7 us (99%)
  local copies, waits for them, and re-layouts  0.64 us (1%)
    pallas_call x1, Pallas kernels, on_device(): pl.pallas_call(kernel, out_shape=jax.ShapeDtypeStruct((PART, d_model), BF...  55.7 us

profile of v5, /device:TPU:1, one launch (start us, length us, event | category | flops | bytes accessed | tf_op | source)
XLA Modules:
  0.0 56.4 jit_solution(1672614316937429283)
XLA Ops:
  0.0 55.7 %layer.1 = bf16[48,1024]{1,0:T(8,128)(2,1)S(1)} custom-call(bf16[192,1024]{1,0:T(8,128)(2,1)} %tok_hbm.1, bf16[1024,128]{1,0:T(8,128)(2,1)} %wq_hbm.1, bf16[1024,128]{1,0:T(8,128)(2,1)} %wk_hbm.1, bf16[1024,128]{1,0:T(8,128)(2,1)} %wv_hbm.1, bf16[128,1024]{1,0:T(8,128)(2,1)} %wo_hbm.1, f32[4]{0:T(128)} %temper_hbm.1), custom_call_target="tpu_custom_call" | custom-call | tf_op jit(solution)/shard_map/layer/pallas_call | solution.py:525
  55.7 0.6 %copy.8 = bf16[48,1024]{1,0:T(8,128)(2,1)} copy(bf16[48,1024]{1,0:T(8,128)(2,1)S(1)} %layer.1) | data formatting | bytes 196608

commit v6 on v5

--- a/solution.py
+++ b/solution.py
@@ -251,7 +251,8 @@
     def _():
         q_copy(0).start()
 
-    q_copy(1).start()
+    for n in (1, 2, 3):
+        q_copy(n).start()
     loads[5].wait()
     w_other.start()
 
@@ -265,9 +266,6 @@
         for g in gathers:
             g.first_got(i)
             g.start(4 * t, 4 * t + 1)
-
-    for n in (2, 3):
-        q_copy(n).start()
 
     def relay(g, t):
         g.got(4 * t)

time: 56.5 us -> 56.8 us (level)
  no operation moved by 1% of the time
where the time goes in v6:
time: 56.8 us; the launch traced here: 56.6 us
  Pallas kernels  56 us (99%)
  local copies, waits for them, and re-layouts  0.64 us (1%)
    pallas_call x1, Pallas kernels, on_device(): pl.pallas_call(kernel, out_shape=jax.ShapeDtypeStruct((PART, d_model), BF...  56 us

profile of v6, /device:TPU:1, one launch (start us, length us, event | category | flops | bytes accessed | tf_op | source)
XLA Modules:
  0.0 56.6 jit_solution(409697212452257301)
XLA Ops:
  0.0 56.0 %layer.1 = bf16[48,1024]{1,0:T(8,128)(2,1)S(1)} custom-call(bf16[192,1024]{1,0:T(8,128)(2,1)} %tok_hbm.1, bf16[1024,128]{1,0:T(8,128)(2,1)} %wq_hbm.1, bf16[1024,128]{1,0:T(8,128)(2,1)} %wk_hbm.1, bf16[1024,128]{1,0:T(8,128)(2,1)} %wv_hbm.1, bf16[128,1024]{1,0:T(8,128)(2,1)} %wo_hbm.1, f32[4]{0:T(128)} %temper_hbm.1), custom_call_target="tpu_custom_call" | custom-call | tf_op jit(solution)/shard_map/layer/pallas_call | solution.py:523
  56.0 0.6 %copy.8 = bf16[48,1024]{1,0:T(8,128)(2,1)} copy(bf16[48,1024]{1,0:T(8,128)(2,1)S(1)} %layer.1) | data formatting | bytes 196608

commit v7 on v6

--- a/solution.py
+++ b/solution.py
@@ -254,7 +254,6 @@
     for n in (1, 2, 3):
         q_copy(n).start()
     loads[5].wait()
-    w_other.start()
 
     @pl.when(jnp.logical_not(mine))
     def _():
@@ -437,6 +436,7 @@
         relay(g, 0)
     for k in range(4):
         q_arrived(k)
+    w_other.start()
     lax.fori_loop(0, 8, step, 0)
 
     w_last.start()

time: 56.8 us -> 56.8 us (level)
  no operation moved by 1% of the time
where the time goes in v7:
time: 56.8 us; the launch traced here: 56.7 us
  Pallas kernels  56 us (99%)
  local copies, waits for them, and re-layouts  0.64 us (1%)
    pallas_call x1, Pallas kernels, on_device(): pl.pallas_call(kernel, out_shape=jax.ShapeDtypeStruct((PART, d_model), BF...  56 us

profile of v7, /device:TPU:1, one launch (start us, length us, event | category | flops | bytes accessed | tf_op | source)
XLA Modules:
  0.0 56.7 jit_solution(11462890563613486015)
XLA Ops:
  0.0 56.0 %layer.1 = bf16[48,1024]{1,0:T(8,128)(2,1)S(1)} custom-call(bf16[192,1024]{1,0:T(8,128)(2,1)} %tok_hbm.1, bf16[1024,128]{1,0:T(8,128)(2,1)} %wq_hbm.1, bf16[1024,128]{1,0:T(8,128)(2,1)} %wk_hbm.1, bf16[1024,128]{1,0:T(8,128)(2,1)} %wv_hbm.1, bf16[128,1024]{1,0:T(8,128)(2,1)} %wo_hbm.1, f32[4]{0:T(128)} %temper_hbm.1), custom_call_target="tpu_custom_call" | custom-call | tf_op jit(solution)/shard_map/layer/pallas_call | solution.py:523
  56.0 0.6 %copy.8 = bf16[48,1024]{1,0:T(8,128)(2,1)} copy(bf16[48,1024]{1,0:T(8,128)(2,1)S(1)} %layer.1) | data formatting | bytes 196608
